TPU v7x, 512 devices: a whole 4x4x16 slice. The times are simulated.
512 devices in a mesh: ctx: 64 (over y, z_lo, core), ch: 8 (over z_hi, x).
Axes of the slice: x: 4, y: 4, z: 16 (z_hi: 2, z_lo: 8; z = z_hi * 8 + z_lo), core: 2. Of those that a mesh axis runs over, the one named last changes fastest.
Arguments:
- x_one: bfloat16 [8192, 4096], P('ctx', 'ch'), may hold values from -6 to 6
- x_two: bfloat16 [8192, 4096], P('ctx', 'ch'), may hold values from -6 to 6
- values: bfloat16 [8192, 4096], P('ctx', 'ch'), may hold values from -6 to 6
- grad_out: bfloat16 [8192, 4096], P('ctx', 'ch'), may hold values from -3 to 3
- filter_raw: bfloat16 [1024, 512], P('ctx', 'ch'), may hold values from -4 to 4
Outputs:
- grad_x_one: bfloat16 [8192, 4096], P('ctx', 'ch')
- grad_x_two: bfloat16 [8192, 4096], P('ctx', 'ch')
- grad_values: bfloat16 [8192, 4096], P('ctx', 'ch')
- grad_filter: float32 [1024, 512], P('ctx', 'ch')
All inputs are finite; a program needn't handle non-finite values.
Results may differ from a plain program's by a relative error of at most 0.0049.
Values may be sent and summed in bfloat16 or wider, within the bound.
A program may use at most 64 MiB of HBM per device.

v0:
```python
import math

import jax
import jax.numpy as jnp
from jax import lax
from jax.sharding import PartitionSpec as P

highest = lax.Precision.HIGHEST


def shifted(value, axis, by):
    peers = lax.axis_size(axis)
    pairs = [(i, i + by) for i in range(peers) if 0 <= i + by < peers]
    return lax.ppermute(value, axis, pairs)


def dft_tables(tok):
    size = 2 * tok
    freq = jnp.arange(tok + 1, dtype=jnp.int32)
    place = jnp.arange(tok, dtype=jnp.int32)

    def angles(rows, cols):
        return 2.0 * math.pi / size * (rows[:, None] * cols[None, :] % size).astype(jnp.float32)

    forward_angle = angles(freq, place)
    forward_table = jnp.concatenate([jnp.cos(forward_angle), -jnp.sin(forward_angle)], axis=0)
    weights = jnp.where((freq == 0) | (freq == tok), 1.0, 2.0).astype(jnp.float32) / size

    def inverse(points):
        angle = angles(points, freq)
        return jnp.concatenate(
            [weights[None, :] * jnp.cos(angle), -weights[None, :] * jnp.sin(angle)], axis=1
        )

    lower_table = inverse(place)
    upper_table = inverse(place + tok)
    lag_table = inverse(tok - place)
    signs = (1 - 2 * (freq % 2)).astype(jnp.float32)
    return (forward_table, lower_table, upper_table, lag_table, signs)


def weigh_plain(fil_real, fil_imag, spec_real, spec_imag):
    real = jnp.sum(fil_real * spec_real - fil_imag * spec_imag, axis=0)
    imag = jnp.sum(fil_real * spec_imag + fil_imag * spec_real, axis=0)
    return (real, imag)


def weigh_conj(fil_real, fil_imag, spec_real, spec_imag):
    real = jnp.sum(fil_real * spec_real + fil_imag * spec_imag, axis=0)
    imag = jnp.sum(fil_real * spec_imag - fil_imag * spec_real, axis=0)
    return (real, imag)


def local(x_one, x_two, values, grad_out, filter_raw):
    tok, chans = x_one.shape
    piece = lax.all_gather(filter_raw, "ctx", axis=0, tiled=True)
    whole = lax.all_gather(piece, "ch", axis=1, tiled=True)
    taps, groups = whole.shape
    span = taps // tok
    repeat = chans // groups
    bins = tok + 1
    scale = 1.0 / math.sqrt(taps)
    forward_table, lower_table, upper_table, lag_table, signs = dft_tables(tok)
    filt = whole.astype(jnp.float32) * scale
    filt_spec = jnp.einsum(
        "mt,ktf->kmf", forward_table, filt.reshape(span, tok, groups), precision=highest
    )
    filt_real = filt_spec[:, :bins, :][:, :, None, :]
    filt_imag = filt_spec[:, bins:, :][:, :, None, :]
    product_in = (x_one.astype(jnp.float32) * values.astype(jnp.float32)).astype(jnp.bfloat16)
    grad_conv = (grad_out.astype(jnp.float32) * x_two.astype(jnp.float32)).astype(jnp.bfloat16)
    lower_list = [product_in]
    upper_list = [grad_conv]
    lower_block = product_in
    upper_block = grad_conv
    for offset in range(1, span + 1):
        lower_block = shifted(lower_block, "ctx", 1)
        upper_block = shifted(upper_block, "ctx", -1)
        lower_list.append(lower_block)
        upper_list.append(upper_block)

    def spectra(blocks):
        stacked = jnp.stack(blocks).astype(jnp.float32)
        spec = jnp.einsum("mt,ktc->kmc", forward_table, stacked, precision=highest)
        return (
            spec[:, :bins].reshape(span + 1, bins, repeat, groups),
            spec[:, bins:].reshape(span + 1, bins, repeat, groups),
        )

    in_real, in_imag = spectra(lower_list)
    grad_real, grad_imag = spectra(upper_list)
    forward_lo = weigh_plain(filt_real, filt_imag, in_real[:span], in_imag[:span])
    forward_hi = weigh_plain(filt_real, filt_imag, in_real[1:], in_imag[1:])
    backward_lo = weigh_conj(filt_real, filt_imag, grad_real[:span], grad_imag[:span])
    backward_hi = weigh_conj(filt_real, filt_imag, grad_real[1:], grad_imag[1:])
    own_real = grad_real[0]
    own_imag = grad_imag[0]
    cross_real = jnp.sum(own_real * in_real + own_imag * in_imag, axis=2)
    cross_imag = jnp.sum(own_real * in_imag - own_imag * in_real, axis=2)

    def inverse_apply(table, parts):
        stacked = jnp.concatenate([parts[0], parts[1]], axis=0).reshape(2 * bins, chans)
        return jnp.dot(table, stacked, precision=highest)

    conv_out = inverse_apply(lower_table, forward_lo) + inverse_apply(upper_table, forward_hi)
    grad_in = inverse_apply(lower_table, backward_lo) + inverse_apply(upper_table, backward_hi)
    grad_x_one = (grad_in * values.astype(jnp.float32)).astype(jnp.bfloat16)
    grad_x_two = (grad_out.astype(jnp.float32) * conv_out).astype(jnp.bfloat16)
    grad_values = (grad_in * x_one.astype(jnp.float32)).astype(jnp.bfloat16)
    lag_real = cross_real[1:] + signs[None, :, None] * cross_real[:-1]
    lag_imag = cross_imag[1:] + signs[None, :, None] * cross_imag[:-1]
    lag_spec = jnp.concatenate([lag_real, lag_imag], axis=1)
    filter_terms = (
        jnp.einsum("rm,kmf->krf", lag_table, lag_spec, precision=highest).reshape(taps, groups)
        * scale
    )
    by_taps = lax.psum_scatter(filter_terms, "ctx", scatter_dimension=0, tiled=True)
    grad_filter = lax.psum_scatter(by_taps, "ch", scatter_dimension=1, tiled=True)
    return (grad_x_one, grad_x_two, grad_values, grad_filter)


def solution(mesh):
    placed = (P("ctx", "ch"), P("ctx", "ch"), P("ctx", "ch"), P("ctx", "ch"), P("ctx", "ch"))
    return jax.shard_map(
        local,
        mesh=mesh,
        in_specs=placed,
        out_specs=(P("ctx", "ch"), P("ctx", "ch"), P("ctx", "ch"), P("ctx", "ch")),
        check_vma=False,
    )
```

profile of v0, /device:TPU:1, one launch (start us, length us, event | category | flops | bytes accessed | tf_op | source)
XLA Modules:
  0.0 816.8 jit_solution(427479515096620973)
XLA Ops:
  8.0 1.0 bitcast_dynamic-update-slice_fusion.8
  9.0 4.9 collective-permute-start.8
  14.0 125.6 %all_gather.6 = bf16[1024,64]{1,0:T(8,128)(2,1)S(1)} all-gather(bf16[16,64]{1,0:T(8,128)(2,1)} %param.9), channel_id=1, replica_groups=mesh['ctx'=64,'ch'=8] {'ctx'}, dimensions={0}, use_global_device_ids=true | all-gather | bytes 133120 | tf_op jit(solution)/shard_map/all_gather | solution.py:56
  139.5 0.8 copy.11
  140.4 1.0 bitcast_dynamic-update-slice_fusion.17
  141.4 2.1 collective-permute-start
  143.5 1.5 sine_multiply_fusion
  145.0 0.3 sine_negate_fusion
  145.3 3.5 collective-permute-start.9
  148.9 1.9 collective-permute-start.1
  150.8 4.3 collective-permute-start.10
  155.1 1.5 collective-permute-done.1
  156.6 1.9 collective-permute-start.2
  158.5 3.6 collective-permute-start.11
  162.2 2.9 collective-permute-done.2
  165.1 1.9 collective-permute-start.3
  167.0 3.6 collective-permute-start.12
  170.7 1.1 collective-permute-done.3
  171.8 1.9 collective-permute-start.4
  173.7 3.6 collective-permute-start.13
  177.4 0.7 collective-permute-done.4
  178.0 1.9 collective-permute-start.5
  180.0 3.6 collective-permute-start.14
  183.7 0.7 collective-permute-done.5
  184.3 1.9 collective-permute-start.6
  186.3 3.6 collective-permute-start.15
  189.9 21.1 %collective-permute-done.6 = bf16[128,512]{1,0:T(8,128)(2,1)S(1)} collective-permute-done((bf16[128,512]{1,0:T(8,128)(2,1)S(1)}, bf16[128,512]{1,0:T(8,128)(2,1)S(1)}, u32[]{:S(2)}, u32[]{:S(2)}) %collective-permute-start.6) | collective-permute-done | bytes 131104 | tf_op jit(solution)/shard_map/ppermute | solution.py:14
  211.0 2.1 collective-permute-start.7
  213.1 4.6 collective-permute-done.7
  217.7 2.3 convolution_bitcast_fusion.1
  220.1 2.4 convolution_bitcast_fusion
  222.5 0.8 multiply_add_fusion
  223.3 1.4 copy-done
  224.7 0.9 fusion.5
  225.6 7.3 fusion.6
  232.9 0.3 reduce-scatter.7.cloned.1.call-start
  233.2 2.9 convert_multiply_fusion
  236.1 1.9 copy.12
  238.0 4.1 convolution_bitcast_fusion.2
  242.2 8.1 subtract_reduce_fusion
  250.3 0.7 fusion.11
  250.9 0.7 fusion.16
  251.6 1.4 fusion.24
  253.0 444.6 %reduce-scatter.5.cloned.1.call-done = f32[16,512]{1,0:T(8,128)} async-done(((f32[1024,512]{1,0:T(8,128)}), f32[16,512]{1,0:T(8,128)}) %reduce-scatter.5.cloned.1.call-update) | async-done | bytes 32784 | tf_op jit(solution)/shard_map/reduce_scatter | solution.py:117
  697.6 1.6 copy.13
  699.3 1.3 fusion.10
  700.6 107.3 %reduce-scatter.7.cloned.1.call-done = f32[64,16]{1,0:T(8,128)} async-done(((f32[512,16]{1,0:T(8,128)}), f32[64,16]{1,0:T(8,128)}) %reduce-scatter.7.cloned.1.call-update) | async-done | bytes 4112
  807.9 1.4 copy.14
  (48 shorter events, 0.4 us)
Async XLA Ops:
  8.0 225.2 %all-gather.2.cloned.1.call-start = ((), (), s32[]{:S(2)}) async-start(), calls=%async_computation.2 | async-start | bytes 1179648 | tf_op jit(solution)/shard_map/all_gather | solution.py:57
  9.0 136.3 %collective-permute-start.8 = (bf16[128,512]{1,0:T(8,128)(2,1)S(1)}, bf16[128,512]{1,0:T(8,128)(2,1)S(1)}, u32[]{:S(2)}, u32[]{:S(2)}) collective-permute-start(bf16[128,512]{1,0:T(8,128)(2,1)S(1)} %get-tuple-element.13), channel_id=1, source_target_pairs={{0,8},{8,16},{16,24},{24,32},{32,40},{40,48},{48,56},{56,64},{64,7... | collective-permute-start | bytes 393224 | tf_op jit(solution)/shard_map/ppermute | solution.py:14
  140.4 557.3 %reduce-scatter.5.cloned.1.call-start = ((), (), s32[]{:S(2)}) async-start(), calls=%async_computation.3 | async-start | bytes 2129920 | tf_op jit(solution)/shard_map/reduce_scatter | solution.py:117
  141.4 7.4 collective-permute-start
  145.3 5.5 collective-permute-start.9
  148.9 7.7 collective-permute-start.1
  150.8 7.7 collective-permute-start.10
  156.6 8.5 %collective-permute-start.2 = (bf16[128,512]{1,0:T(8,128)(2,1)S(1)}, bf16[128,512]{1,0:T(8,128)(2,1)S(1)}, u32[]{:S(2)}, u32[]{:S(2)}) collective-permute-start(bf16[128,512]{1,0:T(8,128)(2,1)S(1)} %collective-permute-done.1), channel_id=1, source_target_pairs={{8,0},{16,8},{24,16},{32,24},{40,32},{48,40},{56,48},{64,56},{72,6... | collective-permute-start | bytes 393224 | tf_op jit(solution)/shard_map/ppermute | solution.py:14
  158.5 8.5 %collective-permute-start.11 = (bf16[128,512]{1,0:T(8,128)(2,1)S(1)}, bf16[128,512]{1,0:T(8,128)(2,1)S(1)}, u32[]{:S(2)}, u32[]{:S(2)}) collective-permute-start(bf16[128,512]{1,0:T(8,128)(2,1)S(1)} %collective-permute-done.10), channel_id=1, source_target_pairs={{0,8},{8,16},{16,24},{24,32},{32,40},{40,48},{48,56},{56,64},{64,7... | collective-permute-start | bytes 393224 | tf_op jit(solution)/shard_map/ppermute | solution.py:14
  165.1 6.7 collective-permute-start.3
  167.0 6.7 collective-permute-start.12
  171.8 6.3 collective-permute-start.4
  173.7 6.3 collective-permute-start.13
  178.0 6.3 collective-permute-start.5
  180.0 6.3 collective-permute-start.14
  184.3 26.7 %collective-permute-start.6 = (bf16[128,512]{1,0:T(8,128)(2,1)S(1)}, bf16[128,512]{1,0:T(8,128)(2,1)S(1)}, u32[]{:S(2)}, u32[]{:S(2)}) collective-permute-start(bf16[128,512]{1,0:T(8,128)(2,1)S(1)} %collective-permute-done.5), channel_id=1, source_target_pairs={{8,0},{16,8},{24,16},{32,24},{40,32},{48,40},{56,48},{64,56},{72,6... | collective-permute-start | bytes 393224 | tf_op jit(solution)/shard_map/ppermute | solution.py:14
  186.3 33.8 %collective-permute-start.15 = (bf16[128,512]{1,0:T(8,128)(2,1)S(1)}, bf16[128,512]{1,0:T(8,128)(2,1)S(1)}, u32[]{:S(2)}, u32[]{:S(2)}) collective-permute-start(bf16[128,512]{1,0:T(8,128)(2,1)S(1)} %collective-permute-done.14), channel_id=1, source_target_pairs={{0,8},{8,16},{16,24},{24,32},{32,40},{40,48},{48,56},{56,64},{64,7... | collective-permute-start | bytes 393224 | tf_op jit(solution)/shard_map/ppermute | solution.py:14
  211.0 6.7 collective-permute-start.7
  220.0 2.5 copy-start.1
  222.5 2.2 copy-start
  232.9 575.1 %reduce-scatter.7.cloned.1.call-start = ((), (), s32[]{:S(2)}) async-start(), calls=%async_computation.4 | async-start | bytes 294912
  242.1 8.1 copy-start.2
  242.1 8.1 copy-start.3
  242.1 9.5 %copy-start.4 = (bf16[128,512]{1,0:T(8,128)(2,1)S(1)}, bf16[128,512]{1,0:T(8,128)(2,1)}, u32[]{:S(2)}) copy-start(bf16[128,512]{1,0:T(8,128)(2,1)} %param.5) | copy-start | bytes 393220
  242.2 9.5 %copy-start.5 = (bf16[128,512]{1,0:T(8,128)(2,1)S(1)}, bf16[128,512]{1,0:T(8,128)(2,1)}, u32[]{:S(2)}) copy-start(bf16[128,512]{1,0:T(8,128)(2,1)} %param.7) | copy-start | bytes 393220
  250.2 449.0 %copy-start.6 = (bf16[128,512]{1,0:T(8,128)(2,1)S(1)}, bf16[128,512]{1,0:T(8,128)(2,1)}, u32[]{:S(2)}) copy-start(bf16[128,512]{1,0:T(8,128)(2,1)} %param.8) | copy-start | bytes 393220
Sparse Core Ops, SparseCore 0:
  140.5 86.8 all-gather.1
  699.4 108.5 reduce-scatter.6
Sparse Core Ops, SparseCore 1:
  232.9 464.6 reduce-scatter.4
where the time goes:
time: 818 us; the launch traced here: 817 us
  waiting for transfers between devices  584 us (71%)
  blocking collectives  126 us (15%)
  starting transfers between devices  46.9 us (6%)
  matrix products  20.1 us (2%)
  other arithmetic  16.4 us (2%)
  between operations  16 us (2%)
    reduce_scatter x1, waiting for transfers between devices, local(): lax.psum_scatter(filter_terms, 'ctx', scatter_dimension=0, tiled=True)  445 us
    all_gather x1, blocking collectives, local(): piece = lax.all_gather(filter_raw, 'ctx', axis=0, tiled=True)  126 us
    unnamed x4, waiting for transfers between devices  107 us
    ppermute x16, starting transfers between devices, shifted(): return lax.ppermute(value, axis, pairs)  46.5 us
    ppermute x16, waiting for transfers between devices, shifted(): return lax.ppermute(value, axis, pairs)  32.4 us
  transfers between devices with their start and end apart: 19, of which 9 were waited for; matrix products, arithmetic and copies ran while one was open for 5% of the time, Pallas kernels for 0%

commit v1 on v0

v1 whole, which is shorter than its diff:
```python
import functools
import math

import jax
import jax.numpy as jnp
from jax import lax
from jax.experimental import pallas as pl
from jax.experimental.pallas import tpu as pltpu
from jax.sharding import PartitionSpec as P

MESH = pl.DeviceIdType.MESH
F32 = jnp.float32
BF16 = jnp.bfloat16
LANES = 128
GROUP = 8


def kernel(
    peers,
    slabs,
    scale,
    x_one_ref,
    x_two_ref,
    values_ref,
    grad_out_ref,
    raw_ref,
    d_one_ref,
    d_two_ref,
    d_values_ref,
    d_filter_ref,
    send_in,
    recv_in,
    send_out,
    recv_out,
    spread,
    prod,
    grad,
    conv_full,
    back_full,
    piece,
    gathered,
    filters,
    taps_rows,
    toeplitz,
    terms,
    term_in,
    term_out,
    owned,
    send_sem,
    recv_sem,
):
    me = lax.axis_index("ctx")
    slab = lax.axis_index("ch")
    tok = x_one_ref.shape[0]
    chans = x_one_ref.shape[1]
    share = peers // slabs
    reach = filters.shape[0] // GROUP
    lead = reach
    mine = me // share
    local_piece = lax.rem(me, share)

    barrier = pltpu.get_barrier_semaphore()

    @pl.loop(1, peers)
    def _(step):
        other = lax.rem(me + step, peers)
        pl.semaphore_signal(barrier, inc=1, device_id={"ctx": other}, device_id_type=MESH)

    @pl.loop(1, slabs)
    def _(step):
        other = lax.rem(slab + step, slabs)
        pl.semaphore_signal(barrier, inc=1, device_id={"ch": other}, device_id_type=MESH)

    @pl.loop(0, share)
    def _(q):
        @pl.when(jnp.logical_or(mine != slab, q != local_piece))
        def _():
            pl.semaphore_signal(
                barrier,
                inc=1,
                device_id={"ctx": slab * share + q, "ch": mine},
                device_id_type=MESH,
            )

    raw = raw_ref[...]
    depth = raw.shape[0]
    row = lax.broadcasted_iota(jnp.int32, (depth, LANES), 0)
    col = lax.broadcasted_iota(jnp.int32, (depth, LANES), 1)
    pick = lax.rem(col, depth) == row
    laid = lax.dot_general(
        raw,
        jnp.where(pick, 1.0, 0.0).astype(BF16),
        (((0,), (0,)), ((), ())),
        preferred_element_type=F32,
    )
    at_row = lax.broadcasted_iota(jnp.int32, laid.shape, 0)
    at_col = lax.broadcasted_iota(jnp.int32, laid.shape, 1)
    own_group = lax.rem(at_row, GROUP) == at_col // depth
    laid = jnp.where(own_group, laid, 0.0)
    piece[...] = jnp.sum(laid.reshape(share, GROUP, LANES), axis=1)

    def lay(left, right):
        product = (left[...].astype(F32) * right[...].astype(F32)).T
        return product.astype(BF16).reshape(peers, GROUP, tok)

    send_in[0] = lay(x_one_ref, values_ref)
    send_in[1] = lay(grad_out_ref, x_two_ref)
    pl.semaphore_wait(barrier, peers - 1 + slabs - 1 + share - jnp.where(mine == slab, 1, 0))

    def copy(src, dst, at, target):
        return pltpu.make_async_remote_copy(
            src_ref=src,
            dst_ref=dst,
            send_sem=send_sem.at[at],
            recv_sem=recv_sem.at[at],
            device_id=target,
            device_id_type=MESH,
        )

    @pl.loop(0, share)
    def _(q):
        @pl.when(jnp.logical_or(mine != slab, q != local_piece))
        def _():
            copy(
                piece.at[pl.ds(q, 1)],
                gathered.at[pl.ds(me, 1)],
                0,
                {"ctx": slab * share + q},
            ).start()

    for which in range(2):

        @pl.loop(1, peers)
        def _(step):
            other = lax.rem(me + step, peers)
            copy(
                send_in.at[which, other], recv_in.at[which, me], 1 + which, {"ctx": other}
            ).start()

    for which in range(2):
        recv_in[which, pl.ds(me, 1)] = send_in[which, pl.ds(me, 1)]

    @pl.when(mine == slab)
    def _():
        gathered[pl.ds(me, 1)] = piece[pl.ds(local_piece, 1)]
        rest = gathered.at[pl.ds(0, peers - 1)]
        copy(rest, rest, 0, {"ctx": me}).wait_recv()

        @pl.loop(1, slabs)
        def _(step):
            other = lax.rem(slab + step, slabs)
            copy(gathered, filters, 3, {"ch": other}).start()

        filters[...] = gathered[...]

        @pl.loop(1, slabs)
        def _(step):
            copy(gathered, filters, 3, {"ch": slab}).wait_send()

    @pl.when(mine != slab)
    def _():
        copy(gathered, filters, 3, {"ch": slab}).wait_recv()

    lane_group = lax.broadcasted_iota(jnp.int32, (reach, LANES), 1) // depth
    sources = [filters[pl.ds(i, reach, stride=GROUP), :] for i in range(GROUP)]
    for c in range(GROUP):
        line = jnp.zeros((reach, LANES), F32)
        for i in range(GROUP):
            turned = pltpu.roll(sources[i], ((i - c) * depth) % LANES, 1)
            line = jnp.where(lane_group == i, turned, line)
        taps_rows[c] = line * scale

    lower = lax.broadcasted_iota(jnp.int32, (LANES, LANES), 0)
    upper = lax.broadcasted_iota(jnp.int32, (LANES, LANES), 1)
    after = upper >= lower
    within = upper <= lower
    flip = jnp.where(upper + lower == LANES - 1, 1.0, 0.0).astype(BF16)

    @pl.loop(0, GROUP)
    def _(c):
        before = jnp.zeros((LANES, LANES), F32)
        for k in range(reach + 1):
            if k < reach:
                line = jnp.broadcast_to(taps_rows[c, pl.ds(k, 1), :], (LANES, LANES))
                turned = pltpu.roll(line, 0, 1, stride=1, stride_axis=0)
            else:
                turned = jnp.zeros((LANES, LANES), F32)
            toeplitz[c, k] = jnp.where(after, turned, before).astype(BF16)
            before = turned

    blocks = reach + 1

    def take_in(which, padded, at):
        rest = recv_in.at[which, pl.ds(0, peers - 1)]
        copy(rest, rest, 1 + which, {"ctx": me}).wait_recv()
        spread[...] = recv_in[which].astype(F32)
        for c in range(GROUP):
            padded[c, pl.ds(at, peers), :] = spread[:, c, :]

    def send_back(which):
        send_out[which] = spread[...].astype(BF16)

        @pl.loop(1, peers)
        def _(step):
            other = lax.rem(me + step, peers)
            copy(
                send_out.at[which, other], recv_out.at[which, me], 4 + which, {"ctx": other}
            ).start()

        recv_out[which, pl.ds(me, 1)] = send_out[which, pl.ds(me, 1)]

    prod[:, pl.ds(0, lead), :] = jnp.zeros((GROUP, lead, LANES), F32)
    grad[:, pl.ds(peers, lead), :] = jnp.zeros((GROUP, lead, LANES), F32)

    take_in(0, prod, lead)

    @pl.loop(0, GROUP)
    def _(c):
        wide = jnp.concatenate(
            [prod[c, pl.ds(lead - k, peers), :].astype(BF16) for k in range(blocks)], axis=1
        )
        tall = jnp.concatenate([toeplitz[c, k] for k in range(blocks)], axis=0)
        conv_full[c] = jnp.dot(wide, tall, preferred_element_type=F32)

    for c in range(GROUP):
        spread[:, c, :] = conv_full[c]
    send_back(0)

    take_in(1, grad, 0)

    @pl.loop(0, GROUP)
    def _(c):
        wide = jnp.concatenate(
            [grad[c, pl.ds(k, peers), :].astype(BF16) for k in range(blocks)], axis=1
        )
        flat = jnp.concatenate([toeplitz[c, k] for k in range(blocks)], axis=1)
        back_full[c] = lax.dot_general(
            wide, flat, (((1,), (1,)), ((), ())), preferred_element_type=F32
        )

    for c in range(GROUP):
        spread[:, c, :] = back_full[c]
    send_back(1)

    @pl.loop(0, GROUP)
    def _(c):
        wide = jnp.concatenate(
            [grad[c, pl.ds(k, peers), :].astype(BF16) for k in range(blocks)], axis=1
        )
        own = prod[c, pl.ds(lead, peers), :].astype(BF16)
        turned_own = lax.dot_general(
            flip, own, (((1,), (1,)), ((), ())), preferred_element_type=F32
        ).astype(BF16)
        cross = jnp.dot(turned_own, wide, preferred_element_type=F32)
        turned = [
            pltpu.roll(cross[:, k * LANES : (k + 1) * LANES], 1, 1, stride=1, stride_axis=0)
            for k in range(blocks)
        ]
        for k in range(reach):
            both = jnp.where(within, turned[k], turned[k + 1])
            terms[k, pl.ds(c, 1), :] = jnp.sum(both, axis=0, keepdims=True)

    @pl.loop(1, slabs)
    def _(step):
        other = lax.rem(slab + step, slabs)
        copy(terms.at[other], term_in.at[slab], 6, {"ch": other}).start()

    term_in[pl.ds(slab, 1)] = terms[pl.ds(slab, 1)]
    rest = term_in.at[pl.ds(0, slabs - 1)]
    copy(rest, rest, 6, {"ch": slab}).wait_recv()
    total = jnp.sum(term_in[...], axis=0) * scale

    at_row = lax.broadcasted_iota(jnp.int32, total.shape, 0)
    at_col = lax.broadcasted_iota(jnp.int32, total.shape, 1) // depth
    crossed = jnp.zeros_like(total)
    for d in range(GROUP):
        moved = total if d == 0 else pltpu.roll(pltpu.roll(total, GROUP - d, 0), d * depth, 1)
        crossed = jnp.where(lax.rem(at_col - at_row + GROUP, GROUP) == d, moved, crossed)
    term_out[...] = crossed

    @pl.loop(0, share)
    def _(q):
        @pl.when(jnp.logical_or(mine != slab, q != local_piece))
        def _():
            copy(
                term_out.at[pl.ds(q, 1)],
                owned.at[pl.ds(local_piece, 1)],
                7,
                {"ctx": slab * share + q, "ch": mine},
            ).start()

    @pl.when(mine == slab)
    def _():
        owned[pl.ds(local_piece, 1)] = term_out[pl.ds(local_piece, 1)]

    def take_out(which):
        rest = recv_out.at[which, pl.ds(0, peers - 1)]
        copy(rest, rest, 4 + which, {"ctx": me}).wait_recv()
        return recv_out[which].astype(F32).reshape(chans, tok).T

    d_two_ref[...] = (take_out(0) * grad_out_ref[...].astype(F32)).astype(BF16)
    back = take_out(1)
    d_one_ref[...] = (back * values_ref[...].astype(F32)).astype(BF16)
    d_values_ref[...] = (back * x_one_ref[...].astype(F32)).astype(BF16)

    @pl.when(mine == slab)
    def _():
        rest = owned.at[pl.ds(0, share - 1)]
        copy(rest, rest, 7, {"ctx": me}).wait()
        rest = gathered.at[pl.ds(0, share - 1)]
        copy(rest, rest, 0, {"ctx": me}).wait_send()

    @pl.when(mine != slab)
    def _():
        copy(owned, owned, 7, {"ctx": me}).wait()
        rest = gathered.at[pl.ds(0, share)]
        copy(rest, rest, 0, {"ctx": me}).wait_send()

    full = jnp.broadcast_to(owned[...][:, None, :], (share, GROUP, LANES))
    full = full.reshape(share * GROUP, LANES)
    full = jnp.where(own_group, full, 0.0)
    d_filter_ref[...] = lax.dot_general(
        jnp.where(pick, 1.0, 0.0),
        full,
        (((1,), (1,)), ((), ())),
        precision=lax.Precision.HIGHEST,
        preferred_element_type=F32,
    )

    for which in range(2):
        rest = send_in.at[which, pl.ds(0, peers - 1)]
        copy(rest, rest, 1 + which, {"ctx": me}).wait_send()
        rest = send_out.at[which, pl.ds(0, peers - 1)]
        copy(rest, rest, 4 + which, {"ctx": me}).wait_send()
    rest = terms.at[pl.ds(0, slabs - 1)]
    copy(rest, rest, 6, {"ch": slab}).wait_send()


def solution(mesh):
    peers = mesh.shape["ctx"]
    slabs = mesh.shape["ch"]

    def local(x_one, x_two, values, grad_out, filter_raw):
        tok, chans = x_one.shape
        depth, owned = filter_raw.shape
        taps = depth * peers
        reach = taps // LANES
        share = peers // slabs
        blocks = reach + 1
        stream = jax.ShapeDtypeStruct((tok, chans), BF16)
        vmem = pl.BlockSpec(memory_space=pltpu.VMEM)
        return pl.pallas_call(
            functools.partial(kernel, peers, slabs, 1.0 / math.sqrt(taps)),
            out_shape=(
                stream,
                stream,
                stream,
                jax.ShapeDtypeStruct((depth, owned), F32),
            ),
            in_specs=[vmem] * 5,
            out_specs=[vmem] * 4,
            scratch_shapes=[
                pltpu.VMEM((2, peers, GROUP, tok), BF16),
                pltpu.VMEM((2, peers, GROUP, tok), BF16),
                pltpu.VMEM((2, peers, GROUP, tok), BF16),
                pltpu.VMEM((2, peers, GROUP, tok), BF16),
                pltpu.VMEM((peers, GROUP, tok), F32),
                pltpu.VMEM((GROUP, peers + reach, tok), F32),
                pltpu.VMEM((GROUP, peers + reach, tok), F32),
                pltpu.VMEM((GROUP, peers, tok), F32),
                pltpu.VMEM((GROUP, peers, tok), F32),
                pltpu.VMEM((share, LANES), F32),
                pltpu.VMEM((peers, LANES), F32),
                pltpu.VMEM((peers, LANES), F32),
                pltpu.VMEM((GROUP, reach, LANES), F32),
                pltpu.VMEM((GROUP, blocks, LANES, LANES), BF16),
                pltpu.VMEM((slabs, GROUP, LANES), F32),
                pltpu.VMEM((slabs, GROUP, LANES), F32),
                pltpu.VMEM((GROUP, LANES), F32),
                pltpu.VMEM((share, LANES), F32),
                pltpu.SemaphoreType.DMA((8,)),
                pltpu.SemaphoreType.DMA((8,)),
            ],
            compiler_params=pltpu.CompilerParams(
                collective_id=0, has_side_effects=True, vmem_limit_bytes=40 * 1024 * 1024
            ),
        )(x_one, x_two, values, grad_out, filter_raw)

    placed = P("ctx", "ch")
    return jax.shard_map(
        local,
        mesh=mesh,
        in_specs=(placed,) * 5,
        out_specs=(placed,) * 4,
        check_vma=False,
    )
```

time: 818 us -> 74.8 us (0.09)
  the two profiles are of different devices: /device:TPU:1 before, /device:TPU:4 now
where the time goes in v1:
time: 74.8 us; the launch traced here: 74.6 us
  Pallas kernels  67.1 us (90%)
  local copies, waits for them, and re-layouts  6.86 us (9%)
    pallas_call x1, Pallas kernels, local(): pl.pallas_call(functools.partial(kernel, peers, slabs, 1.0 / math.sqrt(ta...  67.1 us
    unnamed x14, local copies, waits for them, and re-layouts  6.86 us

profile of v1, /device:TPU:4, one launch (start us, length us, event | category | flops | bytes accessed | tf_op | source)
XLA Modules:
  0.0 74.6 jit_solution(10950897674027029700)
XLA Ops:
  0.6 0.0 copy-start
  0.6 0.9 %copy-done = bf16[128,512]{1,0:T(8,128)(2,1)S(1)} copy-done((bf16[128,512]{1,0:T(8,128)(2,1)S(1)}, bf16[128,512]{1,0:T(8,128)(2,1)}, u32[]{:S(2)}) %copy-start) | copy-done | bytes 131096
  1.5 0.0 copy-start.1
  1.5 0.9 %copy-done.1 = bf16[128,512]{1,0:T(8,128)(2,1)S(1)} copy-done((bf16[128,512]{1,0:T(8,128)(2,1)S(1)}, bf16[128,512]{1,0:T(8,128)(2,1)}, u32[]{:S(2)}) %copy-start.1) | copy-done | bytes 131096
  2.4 0.0 copy-start.2
  2.4 0.9 %copy-done.2 = bf16[128,512]{1,0:T(8,128)(2,1)S(1)} copy-done((bf16[128,512]{1,0:T(8,128)(2,1)S(1)}, bf16[128,512]{1,0:T(8,128)(2,1)}, u32[]{:S(2)}) %copy-start.2) | copy-done | bytes 131096
  3.3 0.0 copy-start.3
  3.3 0.9 %copy-done.3 = bf16[128,512]{1,0:T(8,128)(2,1)S(1)} copy-done((bf16[128,512]{1,0:T(8,128)(2,1)S(1)}, bf16[128,512]{1,0:T(8,128)(2,1)}, u32[]{:S(2)}) %copy-start.3) | copy-done | bytes 131096
  4.3 0.0 copy-start.4
  4.3 0.7 copy-done.4
  4.9 67.1 %shard_map.84 = (bf16[128,512]{1,0:T(8,128)(2,1)S(1)}, bf16[128,512]{1,0:T(8,128)(2,1)S(1)}, bf16[128,512]{1,0:T(8,128)(2,1)S(1)}, f32[16,64]{1,0:T(8,128)S(1)}) custom-call(bf16[128,512]{1,0:T(8,128)(2,1)S(1)} %copy-done, bf16[128,512]{1,0:T(8,128)(2,1)S(1)} %copy-done.1, bf16[128,512]{1,0:T(8,128)(2,1)S(1)} %copy-done.2, bf16[128,512]{1,0:T(8,128)(2,1)S(1)} %copy-done.3, ...), custom_call_target="tpu_custom_call" | custom-call | tf_op jit(solution)/shard_map/pallas_call | solution.py:352
  72.0 0.7 copy.13
  72.7 0.7 copy.14
  73.3 0.7 copy.15
  74.0 0.6 copy.16
Async XLA Ops:
  0.6 0.9 %copy-start = (bf16[128,512]{1,0:T(8,128)(2,1)S(1)}, bf16[128,512]{1,0:T(8,128)(2,1)}, u32[]{:S(2)}) copy-start(bf16[128,512]{1,0:T(8,128)(2,1)} %x_one_ref.1) | copy-start | bytes 393220
  1.5 0.9 %copy-start.1 = (bf16[128,512]{1,0:T(8,128)(2,1)S(1)}, bf16[128,512]{1,0:T(8,128)(2,1)}, u32[]{:S(2)}) copy-start(bf16[128,512]{1,0:T(8,128)(2,1)} %x_two_ref.1) | copy-start | bytes 393220
  2.4 0.9 %copy-start.2 = (bf16[128,512]{1,0:T(8,128)(2,1)S(1)}, bf16[128,512]{1,0:T(8,128)(2,1)}, u32[]{:S(2)}) copy-start(bf16[128,512]{1,0:T(8,128)(2,1)} %values_ref.1) | copy-start | bytes 393220
  3.3 0.9 %copy-start.3 = (bf16[128,512]{1,0:T(8,128)(2,1)S(1)}, bf16[128,512]{1,0:T(8,128)(2,1)}, u32[]{:S(2)}) copy-start(bf16[128,512]{1,0:T(8,128)(2,1)} %grad_out_ref.1) | copy-start | bytes 393220
  4.3 0.7 copy-start.4

commit v2 on v1

v2 whole, which is shorter than its diff:
```python
import functools
import math

import jax
import jax.numpy as jnp
from jax import lax
from jax.experimental import pallas as pl
from jax.experimental.pallas import tpu as pltpu
from jax.sharding import PartitionSpec as P

MESH = pl.DeviceIdType.MESH
F32 = jnp.float32
BF16 = jnp.bfloat16
LANES = 128
GROUP = 8


def kernel(
    peers,
    slabs,
    scale,
    x_one_in,
    x_two_in,
    values_in,
    grad_out_in,
    raw_in,
    d_one_ref,
    d_two_ref,
    d_values_ref,
    d_filter_ref,
    x_one_ref,
    x_two_ref,
    values_ref,
    grad_out_ref,
    raw_ref,
    send_in,
    recv_in,
    send_out,
    recv_out,
    spread,
    prod,
    grad,
    conv_full,
    back_full,
    piece,
    gathered,
    taps_rows,
    toeplitz,
    terms,
    term_out,
    owned,
    load_sem,
    send_sem,
    recv_sem,
):
    me = lax.axis_index("ctx")
    slab = lax.axis_index("ch")
    tok = x_one_ref.shape[0]
    chans = x_one_ref.shape[1]
    share = peers // slabs
    reach = taps_rows.shape[1]
    lead = reach
    blocks = reach + 1
    mine = me // share
    local_piece = lax.rem(me, share)
    at_home = mine == slab

    loads = [
        pltpu.make_async_copy(src, dst, load_sem.at[n])
        for n, (src, dst) in enumerate(
            (
                (x_one_in, x_one_ref),
                (values_in, values_ref),
                (grad_out_in, grad_out_ref),
                (x_two_in, x_two_ref),
                (raw_in, raw_ref),
            )
        )
    ]
    for load in loads:
        load.start()

    barrier = pltpu.get_barrier_semaphore()

    def greet(target):
        pl.semaphore_signal(barrier, inc=1, device_id=target, device_id_type=MESH)

    @pl.loop(0, share * (slabs - 1))
    def _(n):
        other = lax.rem(slab + 1 + n // share, slabs)
        greet({"ctx": slab * share + lax.rem(n, share), "ch": other})

    @pl.when(jnp.logical_not(at_home))
    def _():
        @pl.loop(0, peers)
        def _(n):
            greet({"ctx": lax.rem(me + n, peers), "ch": mine})

    @pl.loop(1, peers)
    def _(step):
        greet({"ctx": lax.rem(me + step, peers)})

    def copy(src, dst, at, target):
        return pltpu.make_async_remote_copy(
            src_ref=src,
            dst_ref=dst,
            send_sem=send_sem.at[at],
            recv_sem=recv_sem.at[at],
            device_id=target,
            device_id_type=MESH,
        )

    def received(ref, count, at):
        rest = ref.at[pl.ds(0, count)]
        copy(rest, rest, at, {"ctx": me}).wait_recv()

    def sent(ref, count, at):
        rest = ref.at[pl.ds(0, count)]
        copy(rest, rest, at, {"ctx": me}).wait_send()

    def by_home(act, ref, at):
        pl.when(at_home)(lambda: act(ref, peers - 1, at))
        pl.when(jnp.logical_not(at_home))(lambda: act(ref, peers, at))

    half = GROUP // 2
    first_half = lax.broadcasted_iota(jnp.int32, (peers, GROUP, tok), 1) < half

    def lay(left, right):
        product = (left[...].astype(F32) * right[...].astype(F32)).T
        return product.reshape(peers, GROUP, tok)

    for load in loads:
        load.wait()
    prods = lay(x_one_ref, values_ref)
    grads = lay(grad_out_ref, x_two_ref)
    send_in[0] = jnp.where(first_half, prods, pltpu.roll(grads, half, 1)).astype(BF16)
    send_in[1] = jnp.where(first_half, pltpu.roll(prods, half, 1), grads).astype(BF16)

    raw = raw_ref[...]
    depth = raw.shape[0]
    row = lax.broadcasted_iota(jnp.int32, (depth, LANES), 0)
    col = lax.broadcasted_iota(jnp.int32, (depth, LANES), 1)
    pick = lax.rem(col, depth) == row
    laid = lax.dot_general(
        raw,
        jnp.where(pick, 1.0, 0.0).astype(BF16),
        (((0,), (0,)), ((), ())),
        preferred_element_type=F32,
    )
    at_row = lax.broadcasted_iota(jnp.int32, laid.shape, 0)
    at_col = lax.broadcasted_iota(jnp.int32, laid.shape, 1)
    own_group = lax.rem(at_row, GROUP) == at_col // depth
    laid = jnp.where(own_group, laid, 0.0)
    piece[...] = jnp.sum(laid.reshape(share, GROUP, LANES), axis=1)

    prod[:, pl.ds(0, lead), :] = jnp.zeros((GROUP, lead, LANES), F32)
    grad[:, pl.ds(peers, lead), :] = jnp.zeros((GROUP, lead, LANES), F32)

    pl.semaphore_wait(
        barrier, peers - 1 + share * (slabs - 1) + jnp.where(at_home, 0, peers)
    )

    def exchange(source, target, part, at):
        @pl.loop(1, peers)
        def _(step):
            other = lax.rem(me + step, peers)
            copy(source.at[part, other], target.at[part, me], at + part, {"ctx": other}).start()

    exchange(send_in, recv_in, 0, 0)

    @pl.loop(0, share * slabs)
    def _(n):
        turn, q = n // share, lax.rem(n, share)
        itself = jnp.logical_and(at_home, jnp.logical_and(turn == 0, q == local_piece))

        @pl.when(jnp.logical_not(itself))
        def _():
            copy(
                piece.at[pl.ds(q, 1)],
                gathered.at[pl.ds(me, 1)],
                4,
                {"ctx": slab * share + q, "ch": lax.rem(slab + turn, slabs)},
            ).start()

    exchange(send_in, recv_in, 1, 0)
    for part in range(2):
        recv_in[part, pl.ds(me, 1)] = send_in[part, pl.ds(me, 1)]

    @pl.when(at_home)
    def _():
        gathered[pl.ds(me, 1)] = piece[pl.ds(local_piece, 1)]

    lower = lax.broadcasted_iota(jnp.int32, (LANES, LANES), 0)
    upper = lax.broadcasted_iota(jnp.int32, (LANES, LANES), 1)
    after = upper >= lower
    within = upper <= lower
    flip = jnp.where(upper + lower == LANES - 1, 1.0, 0.0).astype(BF16)

    def take_in(part):
        received(recv_in.at[part], peers - 1, part)
        spread[...] = recv_in[part].astype(F32)
        for c in range(half):
            prod[part * half + c, pl.ds(lead, peers), :] = spread[:, c, :]
            grad[part * half + c, pl.ds(0, peers), :] = spread[:, half + c, :]

    def correlate(part):
        @pl.loop(part * half, part * half + half)
        def _(c):
            wide = jnp.concatenate(
                [grad[c, pl.ds(k, peers), :].astype(BF16) for k in range(blocks)], axis=1
            )
            own = prod[c, pl.ds(lead, peers), :].astype(BF16)
            turned_own = lax.dot_general(
                flip, own, (((1,), (1,)), ((), ())), preferred_element_type=F32
            ).astype(BF16)
            cross = jnp.dot(turned_own, wide, preferred_element_type=F32)
            turned = [
                pltpu.roll(cross[:, k * LANES : (k + 1) * LANES], 1, 1, stride=1, stride_axis=0)
                for k in range(blocks)
            ]
            for k in range(reach):
                both = jnp.where(within, turned[k], turned[k + 1])
                terms[k, pl.ds(c, 1), :] = jnp.sum(both, axis=0, keepdims=True)

    def convolve(part):
        @pl.loop(part * half, part * half + half)
        def _(c):
            wide = jnp.concatenate(
                [prod[c, pl.ds(lead - k, peers), :].astype(BF16) for k in range(blocks)], axis=1
            )
            tall = jnp.concatenate([toeplitz[c, k] for k in range(blocks)], axis=0)
            conv_full[c] = jnp.dot(wide, tall, preferred_element_type=F32)
            wide = jnp.concatenate(
                [grad[c, pl.ds(k, peers), :].astype(BF16) for k in range(blocks)], axis=1
            )
            flat = jnp.concatenate([toeplitz[c, k] for k in range(blocks)], axis=1)
            back_full[c] = lax.dot_general(
                wide, flat, (((1,), (1,)), ((), ())), preferred_element_type=F32
            )

        for c in range(half):
            spread[:, c, :] = conv_full[part * half + c]
            spread[:, half + c, :] = back_full[part * half + c]
        send_out[part] = spread[...].astype(BF16)
        exchange(send_out, recv_out, part, 2)
        recv_out[part, pl.ds(me, 1)] = send_out[part, pl.ds(me, 1)]

    take_in(0)
    correlate(0)

    by_home(received, gathered, 4)
    lane_group = lax.broadcasted_iota(jnp.int32, (reach, LANES), 1) // depth
    sources = [gathered[pl.ds(i, reach, stride=GROUP), :] for i in range(GROUP)]
    for c in range(GROUP):
        line = jnp.zeros((reach, LANES), F32)
        for i in range(GROUP):
            turned = pltpu.roll(sources[i], ((i - c) * depth) % LANES, 1)
            line = jnp.where(lane_group == i, turned, line)
        taps_rows[c] = line * scale

    @pl.loop(0, GROUP)
    def _(c):
        before = jnp.zeros((LANES, LANES), F32)
        for k in range(blocks):
            if k < reach:
                line = jnp.broadcast_to(taps_rows[c, pl.ds(k, 1), :], (LANES, LANES))
                turned = pltpu.roll(line, 0, 1, stride=1, stride_axis=0)
            else:
                turned = jnp.zeros((LANES, LANES), F32)
            toeplitz[c, k] = jnp.where(after, turned, before).astype(BF16)
            before = turned

    convolve(0)
    take_in(1)
    convolve(1)
    correlate(1)

    total = terms[...] * scale
    at_col = lax.broadcasted_iota(jnp.int32, total.shape, 2) // depth
    at_line = lax.broadcasted_iota(jnp.int32, total.shape, 1)
    crossed = jnp.zeros_like(total)
    for d in range(GROUP):
        moved = total if d == 0 else pltpu.roll(pltpu.roll(total, GROUP - d, 1), d * depth, 2)
        crossed = jnp.where(lax.rem(at_col - at_line + GROUP, GROUP) == d, moved, crossed)
    term_out[...] = crossed.reshape(peers, LANES)
    place = local_piece * slabs + slab

    @pl.loop(0, peers)
    def _(n):
        @pl.when(jnp.logical_or(jnp.logical_not(at_home), n > 0))
        def _():
            other = lax.rem(me + n, peers)
            copy(
                term_out.at[pl.ds(other, 1)],
                owned.at[pl.ds(place, 1)],
                5,
                {"ctx": other, "ch": mine},
            ).start()

    @pl.when(at_home)
    def _():
        owned[pl.ds(place, 1)] = term_out[pl.ds(me, 1)]

    for part in range(2):
        received(recv_out.at[part], peers - 1, 2 + part)
    lead_half = recv_out[0].astype(F32)
    tail_half = recv_out[1].astype(F32)
    conv = jnp.where(first_half, lead_half, pltpu.roll(tail_half, half, 1))
    back = jnp.where(first_half, pltpu.roll(lead_half, half, 1), tail_half)
    conv = conv.reshape(chans, tok).T
    back = back.reshape(chans, tok).T
    d_two_ref[...] = (conv * grad_out_ref[...].astype(F32)).astype(BF16)
    d_one_ref[...] = (back * values_ref[...].astype(F32)).astype(BF16)
    d_values_ref[...] = (back * x_one_ref[...].astype(F32)).astype(BF16)

    by_home(received, owned, 5)
    full = jnp.sum(owned[...].reshape(share, slabs, LANES), axis=1)
    full = jnp.broadcast_to(full[:, None, :], (share, GROUP, LANES))
    full = full.reshape(share * GROUP, LANES)
    full = jnp.where(own_group, full, 0.0)
    d_filter_ref[...] = lax.dot_general(
        jnp.where(pick, 1.0, 0.0),
        full,
        (((1,), (1,)), ((), ())),
        precision=lax.Precision.HIGHEST,
        preferred_element_type=F32,
    )

    for part in range(2):
        sent(send_in.at[part], peers - 1, part)
        sent(send_out.at[part], peers - 1, 2 + part)
    by_home(sent, gathered, 4)
    by_home(sent, owned, 5)


def flush(*refs):
    count = len(refs) // 2
    sem = refs[-1]
    moves = [
        pltpu.make_async_copy(refs[n], refs[count + n], sem.at[n]) for n in range(count)
    ]
    for move in moves:
        move.start()
    for move in moves:
        move.wait()


def solution(mesh):
    peers = mesh.shape["ctx"]
    slabs = mesh.shape["ch"]

    def local(x_one, x_two, values, grad_out, filter_raw):
        tok, chans = x_one.shape
        depth, owned = filter_raw.shape
        taps = depth * peers
        reach = taps // LANES
        share = peers // slabs
        blocks = reach + 1
        stream = jax.ShapeDtypeStruct((tok, chans), BF16)
        shapes = (stream, stream, stream, jax.ShapeDtypeStruct((depth, owned), F32))
        vmem = pl.BlockSpec(memory_space=pltpu.VMEM)
        hbm = pl.BlockSpec(memory_space=pltpu.HBM)
        x_one, x_two, values, grad_out, filter_raw = (
            pltpu.with_memory_space_constraint(a, pltpu.HBM)
            for a in (x_one, x_two, values, grad_out, filter_raw)
        )
        results = pl.pallas_call(
            functools.partial(kernel, peers, slabs, 1.0 / math.sqrt(taps)),
            out_shape=shapes,
            in_specs=[hbm] * 5,
            out_specs=[vmem] * 4,
            scratch_shapes=[
                pltpu.VMEM((tok, chans), BF16),
                pltpu.VMEM((tok, chans), BF16),
                pltpu.VMEM((tok, chans), BF16),
                pltpu.VMEM((tok, chans), BF16),
                pltpu.VMEM((depth, owned), BF16),
                pltpu.VMEM((2, peers, GROUP, tok), BF16),
                pltpu.VMEM((2, peers, GROUP, tok), BF16),
                pltpu.VMEM((2, peers, GROUP, tok), BF16),
                pltpu.VMEM((2, peers, GROUP, tok), BF16),
                pltpu.VMEM((peers, GROUP, tok), F32),
                pltpu.VMEM((GROUP, peers + reach, tok), F32),
                pltpu.VMEM((GROUP, peers + reach, tok), F32),
                pltpu.VMEM((GROUP, peers, tok), F32),
                pltpu.VMEM((GROUP, peers, tok), F32),
                pltpu.VMEM((share, LANES), F32),
                pltpu.VMEM((peers, LANES), F32),
                pltpu.VMEM((GROUP, reach, LANES), F32),
                pltpu.VMEM((GROUP, blocks, LANES, LANES), BF16),
                pltpu.VMEM((reach, GROUP, LANES), F32),
                pltpu.VMEM((peers, LANES), F32),
                pltpu.VMEM((peers, LANES), F32),
                pltpu.SemaphoreType.DMA((5,)),
                pltpu.SemaphoreType.DMA((6,)),
                pltpu.SemaphoreType.DMA((6,)),
            ],
            compiler_params=pltpu.CompilerParams(
                collective_id=0, has_side_effects=True, vmem_limit_bytes=40 * 1024 * 1024
            ),
        )(x_one, x_two, values, grad_out, filter_raw)
        return pl.pallas_call(
            flush,
            out_shape=shapes,
            in_specs=[vmem] * 4,
            out_specs=[hbm] * 4,
            scratch_shapes=[pltpu.SemaphoreType.DMA((4,))],
            compiler_params=pltpu.CompilerParams(vmem_limit_bytes=8 * 1024 * 1024),
        )(*results)

    placed = P("ctx", "ch")
    return jax.shard_map(
        local,
        mesh=mesh,
        in_specs=(placed,) * 5,
        out_specs=(placed,) * 4,
        check_vma=False,
    )
```

time: 74.8 us -> 61.2 us (0.82)
  the two profiles are of different devices: /device:TPU:4 before, /device:TPU:1 now
where the time goes in v2:
time: 61.2 us; the launch traced here: 61.1 us
  Pallas kernels  60.4 us (99%)
  between operations  0.64 us (1%)
    pallas_call x1, Pallas kernels, local(): pl.pallas_call(functools.partial(kernel, peers, slabs, 1.0 / math.sqrt(ta...  59.6 us

profile of v2, /device:TPU:1, one launch (start us, length us, event | category | flops | bytes accessed | tf_op | source)
XLA Modules:
  0.0 61.1 jit_solution(13144933058216208317)
XLA Ops:
  0.6 59.6 %shard_map.84 = (bf16[128,512]{1,0:T(8,128)(2,1)S(1)}, bf16[128,512]{1,0:T(8,128)(2,1)S(1)}, bf16[128,512]{1,0:T(8,128)(2,1)S(1)}, f32[16,64]{1,0:T(8,128)S(1)}) custom-call(bf16[128,512]{1,0:T(8,128)(2,1)} %x_one_in.1, bf16[128,512]{1,0:T(8,128)(2,1)} %x_two_in.1, bf16[128,512]{1,0:T(8,128)(2,1)} %values_in.1, bf16[128,512]{1,0:T(8,128)(2,1)} %grad_out_in.1, ...), custom_call_target="tpu_custom_call" | custom-call | tf_op jit(solution)/shard_map/pallas_call | solution.py:367
  60.3 0.8 %shard_map.85 = (bf16[128,512]{1,0:T(8,128)(2,1)}, bf16[128,512]{1,0:T(8,128)(2,1)}, bf16[128,512]{1,0:T(8,128)(2,1)}, f32[16,64]{1,0:T(8,128)}) custom-call(bf16[128,512]{1,0:T(8,128)(2,1)S(1)} %get-tuple-element.8.refs_0_, bf16[128,512]{1,0:T(8,128)(2,1)S(1)} %get-tuple-element.9.refs_1_, bf16[128,512]{1,0:T(8,128)(2,1)S(1)} %get-tuple-element.10.refs_2_, ...), custom_call_target="tpu_custom_call" | custom-call | tf_op jit(solution)/shard_map/pallas_call | solution.py:402

commit v3 on v2

--- a/solution.py
+++ b/solution.py
@@ -166,8 +166,6 @@
             other = lax.rem(me + step, peers)
             copy(source.at[part, other], target.at[part, me], at + part, {"ctx": other}).start()
 
-    exchange(send_in, recv_in, 0, 0)
-
     @pl.loop(0, share * slabs)
     def _(n):
         turn, q = n // share, lax.rem(n, share)
@@ -182,6 +180,7 @@
                 {"ctx": slab * share + q, "ch": lax.rem(slab + turn, slabs)},
             ).start()
 
+    exchange(send_in, recv_in, 0, 0)
     exchange(send_in, recv_in, 1, 0)
     for part in range(2):
         recv_in[part, pl.ds(me, 1)] = send_in[part, pl.ds(me, 1)]
@@ -245,9 +244,6 @@
         exchange(send_out, recv_out, part, 2)
         recv_out[part, pl.ds(me, 1)] = send_out[part, pl.ds(me, 1)]
 
-    take_in(0)
-    correlate(0)
-
     by_home(received, gathered, 4)
     lane_group = lax.broadcasted_iota(jnp.int32, (reach, LANES), 1) // depth
     sources = [gathered[pl.ds(i, reach, stride=GROUP), :] for i in range(GROUP)]
@@ -270,9 +266,10 @@
             toeplitz[c, k] = jnp.where(after, turned, before).astype(BF16)
             before = turned
 
+    take_in(0)
     convolve(0)
+    correlate(0)
     take_in(1)
-    convolve(1)
     correlate(1)
 
     total = terms[...] * scale
@@ -300,6 +297,8 @@
     @pl.when(at_home)
     def _():
         owned[pl.ds(place, 1)] = term_out[pl.ds(me, 1)]
+
+    convolve(1)
 
     for part in range(2):
         received(recv_out.at[part], peers - 1, 2 + part)

time: 61.2 us -> 55.8 us (0.912)
  Pallas kernels: 60.4 us -> 55 us
    pallas_call x1, Pallas kernels: 59.6 us -> 54.2 us  [local(): pl.pallas_call(functools.partial(kernel, peers, slabs, 1.0 / math.sqrt(ta...]
where the time goes in v3:
time: 55.8 us; the launch traced here: 55.7 us
  Pallas kernels  55 us (99%)
  between operations  0.64 us (1%)
    pallas_call x1, Pallas kernels, local(): pl.pallas_call(functools.partial(kernel, peers, slabs, 1.0 / math.sqrt(ta...  54.2 us

profile of v3, /device:TPU:1, one launch (start us, length us, event | category | flops | bytes accessed | tf_op | source)
XLA Modules:
  0.0 55.7 jit_solution(16474974462945916224)
XLA Ops:
  0.6 54.2 %shard_map.84 = (bf16[128,512]{1,0:T(8,128)(2,1)S(1)}, bf16[128,512]{1,0:T(8,128)(2,1)S(1)}, bf16[128,512]{1,0:T(8,128)(2,1)S(1)}, f32[16,64]{1,0:T(8,128)S(1)}) custom-call(bf16[128,512]{1,0:T(8,128)(2,1)} %x_one_in.1, bf16[128,512]{1,0:T(8,128)(2,1)} %x_two_in.1, bf16[128,512]{1,0:T(8,128)(2,1)} %values_in.1, bf16[128,512]{1,0:T(8,128)(2,1)} %grad_out_in.1, ...), custom_call_target="tpu_custom_call" | custom-call | tf_op jit(solution)/shard_map/pallas_call | solution.py:366
  54.9 0.8 %shard_map.85 = (bf16[128,512]{1,0:T(8,128)(2,1)}, bf16[128,512]{1,0:T(8,128)(2,1)}, bf16[128,512]{1,0:T(8,128)(2,1)}, f32[16,64]{1,0:T(8,128)}) custom-call(bf16[128,512]{1,0:T(8,128)(2,1)S(1)} %get-tuple-element.8.refs_0_, bf16[128,512]{1,0:T(8,128)(2,1)S(1)} %get-tuple-element.9.refs_1_, bf16[128,512]{1,0:T(8,128)(2,1)S(1)} %get-tuple-element.10.refs_2_, ...), custom_call_target="tpu_custom_call" | custom-call | tf_op jit(solution)/shard_map/pallas_call | solution.py:401

commit v4 on v3

--- a/solution.py
+++ b/solution.py
@@ -85,18 +85,13 @@
     def greet(target):
         pl.semaphore_signal(barrier, inc=1, device_id=target, device_id_type=MESH)
 
-    @pl.loop(0, share * (slabs - 1))
-    def _(n):
-        other = lax.rem(slab + 1 + n // share, slabs)
-        greet({"ctx": slab * share + lax.rem(n, share), "ch": other})
-
     @pl.when(jnp.logical_not(at_home))
     def _():
-        @pl.loop(0, peers)
+        @pl.loop(0, peers, unroll=7)
         def _(n):
             greet({"ctx": lax.rem(me + n, peers), "ch": mine})
 
-    @pl.loop(1, peers)
+    @pl.loop(1, peers, unroll=7)
     def _(step):
         greet({"ctx": lax.rem(me + step, peers)})
 
@@ -156,9 +151,7 @@
     prod[:, pl.ds(0, lead), :] = jnp.zeros((GROUP, lead, LANES), F32)
     grad[:, pl.ds(peers, lead), :] = jnp.zeros((GROUP, lead, LANES), F32)
 
-    pl.semaphore_wait(
-        barrier, peers - 1 + share * (slabs - 1) + jnp.where(at_home, 0, peers)
-    )
+    pl.semaphore_wait(barrier, peers - 1 + share * (slabs - 1))
 
     def exchange(source, target, part, at):
         @pl.loop(1, peers)
@@ -203,7 +196,7 @@
             grad[part * half + c, pl.ds(0, peers), :] = spread[:, half + c, :]
 
     def correlate(part):
-        @pl.loop(part * half, part * half + half)
+        @pl.loop(part * half, part * half + half, unroll=2)
         def _(c):
             wide = jnp.concatenate(
                 [grad[c, pl.ds(k, peers), :].astype(BF16) for k in range(blocks)], axis=1
@@ -222,7 +215,7 @@
                 terms[k, pl.ds(c, 1), :] = jnp.sum(both, axis=0, keepdims=True)
 
     def convolve(part):
-        @pl.loop(part * half, part * half + half)
+        @pl.loop(part * half, part * half + half, unroll=2)
         def _(c):
             wide = jnp.concatenate(
                 [prod[c, pl.ds(lead - k, peers), :].astype(BF16) for k in range(blocks)], axis=1
@@ -254,7 +247,7 @@
             line = jnp.where(lane_group == i, turned, line)
         taps_rows[c] = line * scale
 
-    @pl.loop(0, GROUP)
+    @pl.loop(0, GROUP, unroll=GROUP)
     def _(c):
         before = jnp.zeros((LANES, LANES), F32)
         for k in range(blocks):

time: 55.8 us -> 53.2 us (0.953)
  Pallas kernels: 55 us -> 52.4 us
    pallas_call x1, Pallas kernels: 54.2 us -> 51.6 us  [local(): pl.pallas_call(functools.partial(kernel, peers, slabs, 1.0 / math.sqrt(ta...]
where the time goes in v4:
time: 53.2 us; the launch traced here: 53 us
  Pallas kernels  52.4 us (98%)
  between operations  0.64 us (1%)
    pallas_call x1, Pallas kernels, local(): pl.pallas_call(functools.partial(kernel, peers, slabs, 1.0 / math.sqrt(ta...  51.6 us

profile of v4, /device:TPU:1, one launch (start us, length us, event | category | flops | bytes accessed | tf_op | source)
XLA Modules:
  0.0 53.0 jit_solution(7381627307318443080)
XLA Ops:
  0.6 51.6 %shard_map.84 = (bf16[128,512]{1,0:T(8,128)(2,1)S(1)}, bf16[128,512]{1,0:T(8,128)(2,1)S(1)}, bf16[128,512]{1,0:T(8,128)(2,1)S(1)}, f32[16,64]{1,0:T(8,128)S(1)}) custom-call(bf16[128,512]{1,0:T(8,128)(2,1)} %x_one_in.1, bf16[128,512]{1,0:T(8,128)(2,1)} %x_two_in.1, bf16[128,512]{1,0:T(8,128)(2,1)} %values_in.1, bf16[128,512]{1,0:T(8,128)(2,1)} %grad_out_in.1, ...), custom_call_target="tpu_custom_call" | custom-call | tf_op jit(solution)/shard_map/pallas_call | solution.py:359
  52.2 0.8 %shard_map.85 = (bf16[128,512]{1,0:T(8,128)(2,1)}, bf16[128,512]{1,0:T(8,128)(2,1)}, bf16[128,512]{1,0:T(8,128)(2,1)}, f32[16,64]{1,0:T(8,128)}) custom-call(bf16[128,512]{1,0:T(8,128)(2,1)S(1)} %get-tuple-element.8.refs_0_, bf16[128,512]{1,0:T(8,128)(2,1)S(1)} %get-tuple-element.9.refs_1_, bf16[128,512]{1,0:T(8,128)(2,1)S(1)} %get-tuple-element.10.refs_2_, ...), custom_call_target="tpu_custom_call" | custom-call | tf_op jit(solution)/shard_map/pallas_call | solution.py:394

commit v5 on v4

--- a/solution.py
+++ b/solution.py
@@ -154,12 +154,12 @@
     pl.semaphore_wait(barrier, peers - 1 + share * (slabs - 1))
 
     def exchange(source, target, part, at):
-        @pl.loop(1, peers)
+        @pl.loop(1, peers, unroll=7)
         def _(step):
             other = lax.rem(me + step, peers)
             copy(source.at[part, other], target.at[part, me], at + part, {"ctx": other}).start()
 
-    @pl.loop(0, share * slabs)
+    @pl.loop(0, share * slabs, unroll=4)
     def _(n):
         turn, q = n // share, lax.rem(n, share)
         itself = jnp.logical_and(at_home, jnp.logical_and(turn == 0, q == local_piece))
@@ -196,7 +196,7 @@
             grad[part * half + c, pl.ds(0, peers), :] = spread[:, half + c, :]
 
     def correlate(part):
-        @pl.loop(part * half, part * half + half, unroll=2)
+        @pl.loop(part * half, part * half + half, unroll=4)
         def _(c):
             wide = jnp.concatenate(
                 [grad[c, pl.ds(k, peers), :].astype(BF16) for k in range(blocks)], axis=1
@@ -215,7 +215,7 @@
                 terms[k, pl.ds(c, 1), :] = jnp.sum(both, axis=0, keepdims=True)
 
     def convolve(part):
-        @pl.loop(part * half, part * half + half, unroll=2)
+        @pl.loop(part * half, part * half + half, unroll=4)
         def _(c):
             wide = jnp.concatenate(
                 [prod[c, pl.ds(lead - k, peers), :].astype(BF16) for k in range(blocks)], axis=1
@@ -275,7 +275,7 @@
     term_out[...] = crossed.reshape(peers, LANES)
     place = local_piece * slabs + slab
 
-    @pl.loop(0, peers)
+    @pl.loop(0, peers, unroll=4)
     def _(n):
         @pl.when(jnp.logical_or(jnp.logical_not(at_home), n > 0))
         def _():

time: 53.2 us -> 52.5 us (0.987)
  Pallas kernels: 52.4 us -> 51.8 us
    pallas_call x1, Pallas kernels: 51.6 us -> 51 us  [local(): pl.pallas_call(functools.partial(kernel, peers, slabs, 1.0 / math.sqrt(ta...]
where the time goes in v5:
time: 52.5 us; the launch traced here: 52.4 us
  Pallas kernels  51.8 us (99%)
  between operations  0.64 us (1%)
    pallas_call x1, Pallas kernels, local(): pl.pallas_call(functools.partial(kernel, peers, slabs, 1.0 / math.sqrt(ta...  51 us

profile of v5, /device:TPU:1, one launch (start us, length us, event | category | flops | bytes accessed | tf_op | source)
XLA Modules:
  0.0 52.4 jit_solution(16701900525648775773)
XLA Ops:
  0.6 51.0 %shard_map.84 = (bf16[128,512]{1,0:T(8,128)(2,1)S(1)}, bf16[128,512]{1,0:T(8,128)(2,1)S(1)}, bf16[128,512]{1,0:T(8,128)(2,1)S(1)}, f32[16,64]{1,0:T(8,128)S(1)}) custom-call(bf16[128,512]{1,0:T(8,128)(2,1)} %x_one_in.1, bf16[128,512]{1,0:T(8,128)(2,1)} %x_two_in.1, bf16[128,512]{1,0:T(8,128)(2,1)} %values_in.1, bf16[128,512]{1,0:T(8,128)(2,1)} %grad_out_in.1, ...), custom_call_target="tpu_custom_call" | custom-call | tf_op jit(solution)/shard_map/pallas_call | solution.py:359
  51.6 0.8 %shard_map.85 = (bf16[128,512]{1,0:T(8,128)(2,1)}, bf16[128,512]{1,0:T(8,128)(2,1)}, bf16[128,512]{1,0:T(8,128)(2,1)}, f32[16,64]{1,0:T(8,128)}) custom-call(bf16[128,512]{1,0:T(8,128)(2,1)S(1)} %get-tuple-element.8.refs_0_, bf16[128,512]{1,0:T(8,128)(2,1)S(1)} %get-tuple-element.9.refs_1_, bf16[128,512]{1,0:T(8,128)(2,1)S(1)} %get-tuple-element.10.refs_2_, ...), custom_call_target="tpu_custom_call" | custom-call | tf_op jit(solution)/shard_map/pallas_call | solution.py:394
